TPU v7x, 32 devices: a whole 2x2x4 slice. The times are simulated.
32 devices in a mesh: gx: 8 (over z, y), gy: 4 (over x, core).
Axes of the slice: x: 2, y: 2, z: 4, core: 2. Of those that a mesh axis runs over, the one named last changes fastest.
Arguments:
- densities: bfloat16 [8, 4, 64, 8192], P('gx', 'gy'), may hold values from -6 to 6
- trials: bfloat16 [8, 4, 64, 256], P('gx', 'gy'), may hold values from -6 to 6
- energies: float32 [8, 4, 64, 8], P('gx', 'gy'), may hold values from 1 to 4
- metric: bfloat16 [1024, 1024], replicated, may hold values from -0.1875 to 0.1875
- pair_local: int32 [8, 4, 6912], P('gx', 'gy'), may hold values from 0 to 63
- pair_remote: int32 [8, 4, 6912], P('gx', 'gy'), may hold values from 0 to 63, as said below
- pair_scale: float32 [8, 4, 6912], P('gx', 'gy'), may hold values from 0.2 to 2
Outputs:
- sigma_first: float32 [8, 4, 64, 256], P('gx', 'gy')
- corrections: bfloat16 [8, 4, 64, 256], P('gx', 'gy')
- sigma_second: float32 [8, 4, 64, 256], P('gx', 'gy')
- theta: float32 [32], replicated
Inputs may be any that keep to these rules, and one draw needn't show every extreme that they name: pair_remote is below 63 in the slots of the bin's own block (p // 768 = 4); in the other slots it takes every value up to 63.
All inputs are finite; a program needn't handle non-finite values.
Results may differ from a plain program's by a relative error of at most 0.0057.
Values may be sent and summed in bfloat16 or wider, within the bound.
A program may use at most 128 MiB of HBM per device.

v0:
```python
import jax
import jax.numpy as jnp
from jax import lax
from jax.sharding import PartitionSpec as P


def extended(block, sides, width):
    for axis, dim in sides:
        count = lax.axis_size(axis)
        forward = [(i, i + 1) for i in range(count - 1)]
        forward.append((count - 1, 0))
        backward = [(target, source) for source, target in forward]
        low = lax.ppermute(
            lax.slice_in_dim(block, block.shape[dim] - width, None, axis=dim), axis, forward
        )
        high = lax.ppermute(lax.slice_in_dim(block, 0, width, axis=dim), axis, backward)
        block = jnp.concatenate([low, block, high], axis=dim)
    return block


def shards(densities, trials, energies, metric, pair_local, pair_remote, pair_scale):
    mols = densities.shape[2]
    states = energies.shape[3]
    aux = metric.shape[0]
    vecs = trials.shape[3] // states
    pairs = pair_local.shape[2]
    cap = pairs // 9
    width = mols * states
    halo_rho, halo_trial = (
        extended(densities, (("gx", 0), ("gy", 1)), 1),
        extended(trials, (("gx", 0), ("gy", 1)), 1),
    )
    local = pair_local[0, 0]
    owner = jnp.arange(pairs, dtype=jnp.int32) // cap
    inner = jnp.where(owner == 4, (local + 1 + pair_remote[0, 0]) % mols, pair_remote[0, 0])
    molecule_ids = jnp.arange(mols, dtype=jnp.int32)
    own_onehot = (local[:, None] == molecule_ids[None, :]).astype(jnp.float32)
    far_onehot = (inner[:, None] == molecule_ids[None, :]).astype(jnp.float32)
    scaled_own = own_onehot * pair_scale[0, 0][:, None]
    weights = jnp.einsum(
        "opi,opj->oij",
        scaled_own.reshape(9, cap, mols),
        far_onehot.reshape(9, cap, mols),
        precision=lax.Precision.HIGHEST,
    )
    weights = weights / jnp.sqrt(jnp.float32(aux))
    proj = jnp.dot(densities.reshape(width, aux), metric, preferred_element_type=jnp.float32)
    proj = proj.astype(jnp.bfloat16)
    near_rho = halo_rho.reshape(9, width, aux)

    def couple(items):
        far_block, weight = items
        dense = lax.dot_general(
            proj, far_block, (((1,), (1,)), ((), ())), preferred_element_type=jnp.float32
        )
        dense = dense.reshape(mols, states, mols, states) * weight[:, None, :, None]
        return dense.reshape(width, width)

    coupled = lax.map(couple, (near_rho, weights))
    energy = energies[0, 0]

    def matvec(halo_field, own):
        near = halo_field.reshape(9, width, vecs).astype(jnp.float32)
        summed = jnp.einsum("oxy,oyv->xv", coupled, near, precision=lax.Precision.HIGHEST)
        return summed.reshape(mols, states, vecs) + energy[:, :, None] * own

    start_vecs = trials[0, 0].astype(jnp.float32).reshape(mols, states, vecs)
    sigma_first = matvec(halo_trial, start_vecs)
    numer, denom = lax.psum(
        (
            jnp.sum(start_vecs * sigma_first, axis=(0, 1)),
            jnp.sum(start_vecs * start_vecs, axis=(0, 1)),
        ),
        ("gx", "gy"),
    )
    theta = numer / denom
    resid = (sigma_first - theta * start_vecs) / jnp.maximum(
        jnp.abs(energy[:, :, None] - theta), 1.0
    )
    total_sq = lax.psum(jnp.sum(resid * resid, axis=(0, 1)), ("gx", "gy"))
    count = mols * states * lax.axis_size("gx") * lax.axis_size("gy")
    corrections = (resid / jnp.sqrt(total_sq / count + 1e-06)).astype(jnp.bfloat16)
    shaped = corrections.reshape(1, 1, mols, states * vecs)
    halo_corr = extended(shaped, (("gx", 0), ("gy", 1)), 1)
    sigma_second = matvec(halo_corr, corrections.astype(jnp.float32))
    out_shape = (1, 1, mols, states * vecs)
    return (sigma_first.reshape(out_shape), shaped, sigma_second.reshape(out_shape), theta)


def solution(mesh):
    return jax.shard_map(
        shards,
        mesh=mesh,
        in_specs=(
            P("gx", "gy", None, None),
            P("gx", "gy", None, None),
            P("gx", "gy", None, None),
            P(),
            P("gx", "gy", None),
            P("gx", "gy", None),
            P("gx", "gy", None),
        ),
        out_specs=(
            P("gx", "gy", None, None),
            P("gx", "gy", None, None),
            P("gx", "gy", None, None),
            P(),
        ),
        check_vma=False,
    )
```

profile of v0, /device:TPU:0, one launch (start us, length us, event | category | flops | bytes accessed | tf_op | source)
XLA Modules:
  0.0 485.5 jit_solution(373004552011709321)
XLA Ops:
  0.7 3.0 collective-permute-start
  3.7 3.1 collective-permute-start.1
  6.8 42.1 %collective-permute-done = bf16[1,1,64,8192]{3,2,1,0:T(8,128)(2,1)S(1)} collective-permute-done((bf16[1,1,64,8192]{3,2,1,0:T(8,128)(2,1)}, bf16[1,1,64,8192]{3,2,1,0:T(8,128)(2,1)S(1)}, u32[]{:S(2)}, u32[]{:S(2)}) %collective-permute-start) | collective-permute-done | bytes 1048608 | tf_op jit(solution)/shard_map/ppermute | solution.py:13
  49.9 2.3 constant_dynamic-update-slice_fusion.2
  53.3 1.7 collective-permute-start.3
  55.0 2.4 collective-permute-start.4
  57.4 3.0 collective-permute-start.5
  62.7 2.5 convolution_convert_fusion
  68.3 1.7 collective-permute-start.7
  70.2 53.9 %collective-permute-done.6 = bf16[3,1,64,256]{3,2,1,0:T(8,128)(2,1)S(1)} collective-permute-done((bf16[3,1,64,256]{3,2,1,0:T(8,128)(2,1)S(1)}, bf16[3,1,64,256]{3,2,1,0:T(8,128)(2,1)S(1)}, u32[]{:S(2)}, u32[]{:S(2)}) %collective-permute-start.6) | collective-permute-done | bytes 98336 | tf_op jit(solution)/shard_map/ppermute | solution.py:13
  126.5 9.3 %pad_maximum_fusion = bf16[3,3,64,8192]{3,2,1,0:T(8,128)(2,1)} fusion(bf16[3,1,64,8192]{3,2,1,0:T(8,128)(2,1)} %collective-permute-done.3, bf16[3,1,64,8192]{3,2,1,0:T(8,128)(2,1)} %constant_dynamic-update-slice_fusion.1, bf16[3,1,64,8192]{3,2,1,0:T(8,128)(2,1)} %collective-permute-done.2), kind=kLoop, calls=%fused_computation.8 | loop fusion | flops 9437184 | bytes 18874368 | tf_op jit(solution)/shard_map/concatenate | solution.py:17
  135.9 15.0 %reshape.118 = bf16[9,512,1024]{2,1,0:T(8,128)(2,1)} reshape(bf16[3,3,64,8192]{3,2,1,0:T(8,128)(2,1)} %pad_maximum_fusion) | data formatting | bytes 18874368 | tf_op jit(solution)/shard_map/reshape | solution.py:49
  150.9 218.5 %while.10 = (s32[]{:T(128)}, f32[9,512,512]{2,1,0:T(8,128)}, bf16[9,512,1024]{2,1,0:T(8,128)(2,1)}, bf16[512,1024]{1,0:T(8,128)(2,1)S(1)}, f32[9,64,64]{2,1,0:T(8,128)S(1)}, /*index=5*/s32[]{:T(128)}) while((s32[]{:T(128)}, f32[9,512,512]{2,1,0:T(8,128)}, bf16[9,512,1024]{2,1,0:T(8,128)(2,1)}, bf16[512,1024]{1,0:T(8,128)(2,1)S(1)}, ...), condition=%wide.region_1.2_spmd, body=%wide.region_0.1_spmd.sunk | while | flops 537133056 | bytes 13681737 | solution.py:59
  150.9 7.9 %mul.110 = f32[64,8,64,8]{3,2,1,0:T(8,128)} broadcast(f32[64,64]{1,0:T(8,128)S(1)} %dynamic-slice_bitcast_fusion.2), dimensions={0,2} | broadcast | bytes 1064960 | tf_op jit(solution)/shard_map/while/body/eval_jaxpr/mul | solution.py:56
  158.8 12.6 %mul.111 = f32[512,512]{1,0:T(8,128)S(1)} reshape(f32[64,8,64,8]{3,2,1,0:T(8,128)} %mul.110) | data formatting | bytes 2097152 | tf_op jit(solution)/shard_map/while/body/eval_jaxpr/mul | solution.py:56
  171.8 2.0 fusion.43
  175.1 7.9 %mul.110 = f32[64,8,64,8]{3,2,1,0:T(8,128)} broadcast(f32[64,64]{1,0:T(8,128)S(1)} %dynamic-slice_bitcast_fusion.2), dimensions={0,2} | broadcast | bytes 1064960 | tf_op jit(solution)/shard_map/while/body/eval_jaxpr/mul | solution.py:56
  183.1 12.6 %mul.111 = f32[512,512]{1,0:T(8,128)S(1)} reshape(f32[64,8,64,8]{3,2,1,0:T(8,128)} %mul.110) | data formatting | bytes 2097152 | tf_op jit(solution)/shard_map/while/body/eval_jaxpr/mul | solution.py:56
  196.0 2.0 fusion.43
  199.4 7.9 %mul.110 = f32[64,8,64,8]{3,2,1,0:T(8,128)} broadcast(f32[64,64]{1,0:T(8,128)S(1)} %dynamic-slice_bitcast_fusion.2), dimensions={0,2} | broadcast | bytes 1064960 | tf_op jit(solution)/shard_map/while/body/eval_jaxpr/mul | solution.py:56
  207.4 12.6 %mul.111 = f32[512,512]{1,0:T(8,128)S(1)} reshape(f32[64,8,64,8]{3,2,1,0:T(8,128)} %mul.110) | data formatting | bytes 2097152 | tf_op jit(solution)/shard_map/while/body/eval_jaxpr/mul | solution.py:56
  220.3 2.0 fusion.43
  223.7 7.9 %mul.110 = f32[64,8,64,8]{3,2,1,0:T(8,128)} broadcast(f32[64,64]{1,0:T(8,128)S(1)} %dynamic-slice_bitcast_fusion.2), dimensions={0,2} | broadcast | bytes 1064960 | tf_op jit(solution)/shard_map/while/body/eval_jaxpr/mul | solution.py:56
  231.6 12.6 %mul.111 = f32[512,512]{1,0:T(8,128)S(1)} reshape(f32[64,8,64,8]{3,2,1,0:T(8,128)} %mul.110) | data formatting | bytes 2097152 | tf_op jit(solution)/shard_map/while/body/eval_jaxpr/mul | solution.py:56
  244.6 2.0 fusion.43
  248.0 7.9 %mul.110 = f32[64,8,64,8]{3,2,1,0:T(8,128)} broadcast(f32[64,64]{1,0:T(8,128)S(1)} %dynamic-slice_bitcast_fusion.2), dimensions={0,2} | broadcast | bytes 1064960 | tf_op jit(solution)/shard_map/while/body/eval_jaxpr/mul | solution.py:56
  255.9 12.6 %mul.111 = f32[512,512]{1,0:T(8,128)S(1)} reshape(f32[64,8,64,8]{3,2,1,0:T(8,128)} %mul.110) | data formatting | bytes 2097152 | tf_op jit(solution)/shard_map/while/body/eval_jaxpr/mul | solution.py:56
  268.8 2.0 fusion.43
  272.2 7.9 %mul.110 = f32[64,8,64,8]{3,2,1,0:T(8,128)} broadcast(f32[64,64]{1,0:T(8,128)S(1)} %dynamic-slice_bitcast_fusion.2), dimensions={0,2} | broadcast | bytes 1064960 | tf_op jit(solution)/shard_map/while/body/eval_jaxpr/mul | solution.py:56
  280.1 12.6 %mul.111 = f32[512,512]{1,0:T(8,128)S(1)} reshape(f32[64,8,64,8]{3,2,1,0:T(8,128)} %mul.110) | data formatting | bytes 2097152 | tf_op jit(solution)/shard_map/while/body/eval_jaxpr/mul | solution.py:56
  293.1 2.0 fusion.43
  296.5 7.9 %mul.110 = f32[64,8,64,8]{3,2,1,0:T(8,128)} broadcast(f32[64,64]{1,0:T(8,128)S(1)} %dynamic-slice_bitcast_fusion.2), dimensions={0,2} | broadcast | bytes 1064960 | tf_op jit(solution)/shard_map/while/body/eval_jaxpr/mul | solution.py:56
  304.4 12.6 %mul.111 = f32[512,512]{1,0:T(8,128)S(1)} reshape(f32[64,8,64,8]{3,2,1,0:T(8,128)} %mul.110) | data formatting | bytes 2097152 | tf_op jit(solution)/shard_map/while/body/eval_jaxpr/mul | solution.py:56
  317.4 2.0 fusion.43
  320.8 7.9 %mul.110 = f32[64,8,64,8]{3,2,1,0:T(8,128)} broadcast(f32[64,64]{1,0:T(8,128)S(1)} %dynamic-slice_bitcast_fusion.2), dimensions={0,2} | broadcast | bytes 1064960 | tf_op jit(solution)/shard_map/while/body/eval_jaxpr/mul | solution.py:56
  328.7 12.6 %mul.111 = f32[512,512]{1,0:T(8,128)S(1)} reshape(f32[64,8,64,8]{3,2,1,0:T(8,128)} %mul.110) | data formatting | bytes 2097152 | tf_op jit(solution)/shard_map/while/body/eval_jaxpr/mul | solution.py:56
  341.6 2.0 fusion.43
  345.0 7.9 %mul.110 = f32[64,8,64,8]{3,2,1,0:T(8,128)} broadcast(f32[64,64]{1,0:T(8,128)S(1)} %dynamic-slice_bitcast_fusion.2), dimensions={0,2} | broadcast | bytes 1064960 | tf_op jit(solution)/shard_map/while/body/eval_jaxpr/mul | solution.py:56
  352.9 12.6 %mul.111 = f32[512,512]{1,0:T(8,128)S(1)} reshape(f32[64,8,64,8]{3,2,1,0:T(8,128)} %mul.110) | data formatting | bytes 2097152 | tf_op jit(solution)/shard_map/while/body/eval_jaxpr/mul | solution.py:56
  365.9 2.0 fusion.43
  369.4 8.1 %fusion.16 = f32[64,8,32]{2,1,0:T(8,128)S(1)} fusion(bf16[9,512,32]{2,1,0:T(8,128)(2,1)} %reshape.120, f32[9,512,512]{2,1,0:T(8,128)} %get-tuple-element.31), kind=kOutput, calls=%fused_computation.21 | convolution fusion | flops 905969664 | bytes 9797632 | tf_op jit(solution)/shard_map/oxy,oyv->xv/dot_general | solution.py:64
  377.8 41.5 %all-reduce = (f32[32]{0:T(128)S(1)}, f32[32]{0:T(128)S(1)}) all-reduce(f32[32]{0:T(128)S(1)} %get-tuple-element.61, f32[32]{0:T(128)S(1)} %reduce_sum.37), channel_id=1, replica_groups=mesh['gx'=8,'gy'=4] {'gx','gy'}, use_global_device_ids=true, to_apply=%region_3.4 | all-reduce | flops 64 | bytes 512 | tf_op jit(solution)/shard_map/psum | solution.py:69
  419.6 40.3 %psum.23 = f32[32]{0:T(128)S(1)} all-reduce(f32[32]{0:T(128)S(1)} %multiply_reduce_fusion), channel_id=1, replica_groups=mesh['gx'=8,'gy'=4] {'gx','gy'}, use_global_device_ids=true, to_apply=%region_8.9 | all-reduce | flops 32 | bytes 256 | tf_op jit(solution)/shard_map/psum | solution.py:80
  460.0 2.3 collective-permute-start.8
  462.3 2.5 collective-permute-start.9
  464.8 2.3 collective-permute-done.8
  470.6 1.9 collective-permute-done.10
  475.0 8.7 %fusion.21 = f32[64,8,32]{2,1,0:T(8,128)} fusion(bf16[9,512,32]{2,1,0:T(8,128)(2,1)S(1)} %reshape.123, f32[9,512,512]{2,1,0:T(8,128)} %get-tuple-element.31), kind=kOutput, calls=%fused_computation.22 | convolution fusion | flops 905969664 | bytes 9797632 | tf_op jit(solution)/shard_map/oxy,oyv->xv/dot_general | solution.py:64
  (104 shorter events, 34.0 us)
Async XLA Ops:
  0.6 62.1 %copy-start = (bf16[1024,1024]{1,0:T(8,128)(2,1)S(1)}, bf16[1024,1024]{1,0:T(8,128)(2,1)}, u32[]{:S(2)}) copy-start(bf16[1024,1024]{1,0:T(8,128)(2,1)} %param.12) | copy-start | bytes 6291460
  0.6 59.8 %copy-start.2 = (bf16[1,1,64,8192]{3,2,1,0:T(8,128)(2,1)S(1)}, bf16[1,1,64,8192]{3,2,1,0:T(8,128)(2,1)}, u32[]{:S(2)}) copy-start(bf16[1,1,64,8192]{3,2,1,0:T(8,128)(2,1)} %param.9) | copy-start | bytes 3145732
  0.7 54.4 %copy-start.3 = (bf16[1,1,64,256]{3,2,1,0:T(8,128)(2,1)S(1)}, bf16[1,1,64,256]{3,2,1,0:T(8,128)(2,1)}, u32[]{:S(2)}) copy-start(bf16[1,1,64,256]{3,2,1,0:T(8,128)(2,1)} %param.10) | copy-start | bytes 98308
  0.7 48.2 %collective-permute-start = (bf16[1,1,64,8192]{3,2,1,0:T(8,128)(2,1)}, bf16[1,1,64,8192]{3,2,1,0:T(8,128)(2,1)S(1)}, u32[]{:S(2)}, u32[]{:S(2)}) collective-permute-start(bf16[1,1,64,8192]{3,2,1,0:T(8,128)(2,1)} %param.9), channel_id=1, source_target_pairs={{0,4},{4,8},{8,12},{12,16},{16,20},{20,24},{24,28},{28,0},{1,5},{5... | collective-permute-start | bytes 3145736 | tf_op jit(solution)/shard_map/ppermute | solution.py:13
  3.7 48.5 %collective-permute-start.1 = (bf16[1,1,64,8192]{3,2,1,0:T(8,128)(2,1)}, bf16[1,1,64,8192]{3,2,1,0:T(8,128)(2,1)S(1)}, u32[]{:S(2)}, u32[]{:S(2)}) collective-permute-start(bf16[1,1,64,8192]{3,2,1,0:T(8,128)(2,1)} %param.9), channel_id=1, source_target_pairs={{4,0},{8,4},{12,8},{16,12},{20,16},{24,20},{28,24},{0,28},{5,1},{9... | collective-permute-start | bytes 3145736 | tf_op jit(solution)/shard_map/ppermute | solution.py:16
  49.9 11.8 %copy-start.6 = (s32[1,1,6912]{2,1,0:T(1,128)S(1)}, s32[1,1,6912]{2,1,0:T(1,128)}, u32[]{:S(2)}) copy-start(s32[1,1,6912]{2,1,0:T(1,128)} %param.13) | copy-start | bytes 82948
  49.9 11.9 %copy-start.7 = (s32[1,1,6912]{2,1,0:T(1,128)S(1)}, s32[1,1,6912]{2,1,0:T(1,128)}, u32[]{:S(2)}) copy-start(s32[1,1,6912]{2,1,0:T(1,128)} %param.14) | copy-start | bytes 82948
  49.9 12.0 %copy-start.8 = (f32[1,1,6912]{2,1,0:T(1,128)S(1)}, f32[1,1,6912]{2,1,0:T(1,128)}, u32[]{:S(2)}) copy-start(f32[1,1,6912]{2,1,0:T(1,128)} %param.15) | copy-start | bytes 82948
  53.3 73.3 %collective-permute-start.2 = (bf16[3,1,64,8192]{3,2,1,0:T(8,128)(2,1)}, bf16[3,1,64,8192]{3,2,1,0:T(8,128)(2,1)}, u32[]{:S(2)}, u32[]{:S(2)}) collective-permute-start(bf16[3,1,64,8192]{3,2,1,0:T(8,128)(2,1)} %constant_dynamic-update-slice_fusion.1), channel_id=1, source_target_pairs={{0,1},{1,2},{2,3},{3,0},{4,5},{5,6},{6,7},{7,4},{8,9},{9,10},{10,1... | collective-permute-start | bytes 9437192 | tf_op jit(solution)/shard_map/ppermute | solution.py:13
  53.3 73.3 %collective-permute-start.3 = (bf16[3,1,64,8192]{3,2,1,0:T(8,128)(2,1)}, bf16[3,1,64,8192]{3,2,1,0:T(8,128)(2,1)}, u32[]{:S(2)}, u32[]{:S(2)}) collective-permute-start(bf16[3,1,64,8192]{3,2,1,0:T(8,128)(2,1)} %constant_dynamic-update-slice_fusion.1), channel_id=1, source_target_pairs={{1,0},{2,1},{3,2},{0,3},{5,4},{6,5},{7,6},{4,7},{9,8},{10,9},{11,1... | collective-permute-start | bytes 9437192 | tf_op jit(solution)/shard_map/ppermute | solution.py:16
  55.0 11.7 %collective-permute-start.4 = (bf16[1,1,64,256]{3,2,1,0:T(8,128)(2,1)S(1)}, bf16[1,1,64,256]{3,2,1,0:T(8,128)(2,1)}, u32[]{:S(2)}, u32[]{:S(2)}) collective-permute-start(bf16[1,1,64,256]{3,2,1,0:T(8,128)(2,1)S(1)} %copy-done.3), channel_id=1, source_target_pairs={{0,4},{4,8},{8,12},{12,16},{16,20},{20,24},{24,28},{28,0},{1,5},{5... | collective-permute-start | bytes 98312 | tf_op jit(solution)/shard_map/ppermute | solution.py:13
  57.4 10.1 %collective-permute-start.5 = (bf16[1,1,64,256]{3,2,1,0:T(8,128)(2,1)S(1)}, bf16[1,1,64,256]{3,2,1,0:T(8,128)(2,1)}, u32[]{:S(2)}, u32[]{:S(2)}) collective-permute-start(bf16[1,1,64,256]{3,2,1,0:T(8,128)(2,1)S(1)} %copy-done.3), channel_id=1, source_target_pairs={{4,0},{8,4},{12,8},{16,12},{20,16},{24,20},{28,24},{0,28},{5,1},{9... | collective-permute-start | bytes 98312 | tf_op jit(solution)/shard_map/ppermute | solution.py:16
  62.7 2.5 copy-start.5
  68.3 55.9 %collective-permute-start.6 = (bf16[3,1,64,256]{3,2,1,0:T(8,128)(2,1)S(1)}, bf16[3,1,64,256]{3,2,1,0:T(8,128)(2,1)S(1)}, u32[]{:S(2)}, u32[]{:S(2)}) collective-permute-start(bf16[3,1,64,256]{3,2,1,0:T(8,128)(2,1)S(1)} %constant_dynamic-update-slice_fusion.4), channel_id=1, source_target_pairs={{0,1},{1,2},{2,3},{3,0},{4,5},{5,6},{6,7},{7,4},{8,9},{9,10},{10,1... | collective-permute-start | bytes 294920 | tf_op jit(solution)/shard_map/ppermute | solution.py:13
  68.3 56.7 %collective-permute-start.7 = (bf16[3,1,64,256]{3,2,1,0:T(8,128)(2,1)S(1)}, bf16[3,1,64,256]{3,2,1,0:T(8,128)(2,1)S(1)}, u32[]{:S(2)}, u32[]{:S(2)}) collective-permute-start(bf16[3,1,64,256]{3,2,1,0:T(8,128)(2,1)S(1)} %constant_dynamic-update-slice_fusion.4), channel_id=1, source_target_pairs={{1,0},{2,1},{3,2},{0,3},{5,4},{6,5},{7,6},{4,7},{9,8},{10,9},{11,1... | collective-permute-start | bytes 294920 | tf_op jit(solution)/shard_map/ppermute | solution.py:16
  369.4 8.3 %copy-start.4 = (f32[1,1,64,8]{2,3,1,0:T(8,128)S(1)}, f32[1,1,64,8]{2,3,1,0:T(8,128)}, u32[]{:S(2)}) copy-start(f32[1,1,64,8]{2,3,1,0:T(8,128)} %param.11) | copy-start | bytes 6148
  419.3 64.4 %copy-start.9 = (f32[32]{0:T(128)}, f32[32]{0:T(128)S(1)}, u32[]{:S(2)}) copy-start(f32[32]{0:T(128)S(1)} %div.39) | copy-start | bytes 388
  460.0 7.1 %collective-permute-start.8 = (bf16[1,1,64,256]{2,3,1,0:T(8,128)(2,1)S(1)}, bf16[1,1,64,256]{2,3,1,0:T(8,128)(2,1)S(1)}, u32[]{:S(2)}, u32[]{:S(2)}) collective-permute-start(bf16[1,1,64,256]{2,3,1,0:T(8,128)(2,1)S(1)} %bitcast.72), channel_id=1, source_target_pairs={{0,4},{4,8},{8,12},{12,16},{16,20},{20,24},{24,28},{28,0},{1,5},{5... | collective-permute-start | bytes 98312 | tf_op jit(solution)/shard_map/ppermute | solution.py:13
  462.3 5.0 %collective-permute-start.9 = (bf16[1,1,64,256]{2,3,1,0:T(8,128)(2,1)S(1)}, bf16[1,1,64,256]{2,3,1,0:T(8,128)(2,1)S(1)}, u32[]{:S(2)}, u32[]{:S(2)}) collective-permute-start(bf16[1,1,64,256]{2,3,1,0:T(8,128)(2,1)S(1)} %bitcast.73), channel_id=1, source_target_pairs={{4,0},{8,4},{12,8},{16,12},{20,16},{24,20},{28,24},{0,28},{5,1},{9... | collective-permute-start | bytes 98312 | tf_op jit(solution)/shard_map/ppermute | solution.py:16
  467.4 5.1 %collective-permute-start.10 = (bf16[3,1,64,256]{2,3,1,0:T(8,128)(2,1)S(1)}, bf16[3,1,64,256]{2,3,1,0:T(8,128)(2,1)S(1)}, u32[]{:S(2)}, u32[]{:S(2)}) collective-permute-start(bf16[3,1,64,256]{2,3,1,0:T(8,128)(2,1)S(1)} %pad_maximum_fusion.3), channel_id=1, source_target_pairs={{0,1},{1,2},{2,3},{3,0},{4,5},{5,6},{6,7},{7,4},{8,9},{9,10},{10,1... | collective-permute-start | bytes 294920 | tf_op jit(solution)/shard_map/ppermute | solution.py:13
  467.4 6.7 %collective-permute-start.11 = (bf16[3,1,64,256]{2,3,1,0:T(8,128)(2,1)S(1)}, bf16[3,1,64,256]{2,3,1,0:T(8,128)(2,1)S(1)}, u32[]{:S(2)}, u32[]{:S(2)}) collective-permute-start(bf16[3,1,64,256]{2,3,1,0:T(8,128)(2,1)S(1)} %pad_maximum_fusion.3), channel_id=1, source_target_pairs={{1,0},{2,1},{3,2},{0,3},{5,4},{6,5},{7,6},{4,7},{9,8},{10,9},{11,1... | collective-permute-start | bytes 294920 | tf_op jit(solution)/shard_map/ppermute | solution.py:16
  475.0 10.5 %copy-start.1 = (bf16[1024,1024]{1,0:T(8,128)(2,1)S(1)}, bf16[1024,1024]{1,0:T(8,128)(2,1)}, u32[]{:S(2)}) copy-start(bf16[1024,1024]{1,0:T(8,128)(2,1)} %param.12) | copy-start | bytes 6291460
where the time goes:
time: 488 us; the launch traced here: 486 us
  local copies, waits for them, and re-layouts  229 us (47%)
  waiting for transfers between devices  103 us (21%)
  blocking collectives  81.9 us (17%)
  matrix products  38.4 us (8%)
  starting transfers between devices  21.6 us (4%)
  other arithmetic  10.5 us (2%)
    mul x36, local copies, waits for them, and re-layouts, couple(): dense = dense.reshape(mols, states, mols, states) * weight[:, None, :, None]  188 us
    ppermute x6, waiting for transfers between devices, extended(): lax.ppermute(lax.slice_in_dim(block, block.shape[dim] - width, None, axis...  100 us
    psum x1, blocking collectives, shards(): lax.psum((jnp.sum(start_vecs * sigma_first, axis=(0, 1)), jnp.sum(start_v...  41.5 us
    psum x1, blocking collectives, shards(): total_sq = lax.psum(jnp.sum(resid * resid, axis=(0, 1)), ('gx', 'gy'))  40.3 us
    dot_general x9, matrix products, couple(): lax.dot_general(proj, far_block, (((1,), (1,)), ((), ())), preferred_elem...  17.7 us
    dot_general x2, matrix products, matvec(): jnp.einsum('oxy,oyv->xv', coupled, near, precision=lax.Precision.HIGHEST)  16.8 us
    reshape x1, local copies, waits for them, and re-layouts, shards(): near_rho = halo_rho.reshape(9, width, aux)  15 us
    ppermute x6, starting transfers between devices, extended(): lax.ppermute(lax.slice_in_dim(block, 0, width, axis=dim), axis, backward)  13.8 us
  transfers between devices with their start and end apart: 12, of which 7 were waited for; matrix products, arithmetic and copies ran while one was open for 3% of the time, Pallas kernels for 0%

commit v1 on v0

v1 whole, which is shorter than its diff:
```python
import functools

import jax
import jax.numpy as jnp
from jax import lax
from jax.experimental import pallas as pl
from jax.experimental.pallas import tpu as pltpu
from jax.sharding import PartitionSpec as P

MESH = pl.DeviceIdType.MESH
NT = (((1,), (1,)), ((), ()))
LANES = 128
F32 = jnp.float32
BF16 = jnp.bfloat16


def kernel(
    nx, ny,
    rho, trial, energy, metric, plocal, premote, pscale,
    sigma_first, corr_out, sigma_second, theta_out,
    near, proj, c_own, c_low, c_left, c_right,
    w_own, w_send, w_low, w_side,
    y_near, r_send, r_near, ycat, ret_send, ret_near, sum_y, sum_x,
    rho_ss, rho_rs, small_ss, small_rs, ysum_ss, ysum_rs, xsum_ss, xsum_rs,
):
    mols, full = rho.shape[2], rho.shape[3]
    aux = metric.shape[0]
    states = full // aux
    vecs = trial.shape[3] // states
    width = mols * states
    cap = plocal.shape[2] // 9
    tile = c_left.shape[1] // 2
    me_x, me_y = lax.axis_index("gx"), lax.axis_index("gy")
    up = (lax.rem(me_x + 1, nx), me_y)
    down = (lax.rem(me_x + nx - 1, nx), me_y)
    right = (me_x, lax.rem(me_y + 1, ny))
    left = (me_x, lax.rem(me_y + ny - 1, ny))
    routes = ((right, 0), (left, 1), (up, 2))

    barrier = pltpu.get_barrier_semaphore()
    for k in range(1, ny):
        pl.semaphore_signal(barrier, inc=1, device_id=(me_x, lax.rem(me_y + k, ny)), device_id_type=MESH)
    for k in range(1, nx):
        pl.semaphore_signal(barrier, inc=1, device_id=(lax.rem(me_x + k, nx), me_y), device_id_type=MESH)
    pl.semaphore_wait(barrier, nx + ny - 2)

    pending = []

    def send(src, dst, ss, rs, target):
        copy = pltpu.make_async_remote_copy(
            src_ref=src, dst_ref=dst, send_sem=ss, recv_sem=rs, device_id=target, device_id_type=MESH
        )
        copy.start()
        pending.append(copy)
        return copy

    y_copies = [
        send(trial.at[0, 0], y_near.at[slot], small_ss.at[0, slot], small_rs.at[0, slot], target)
        for target, slot in routes
    ]
    rho_copies = [[None] * states for _ in range(3)]
    for a in range(states):
        for target, slot in routes:
            rho_copies[slot][a] = send(
                rho.at[0, 0, :, pl.ds(a * aux, aux)],
                near.at[pl.ds((slot + 1) * width + a * mols, mols), :],
                rho_ss.at[slot, a], rho_rs.at[slot, a], target,
            )

    norm = 1.0 / (float(aux) ** 0.5)
    ids = lax.broadcasted_iota(jnp.int32, (mols, cap), 0)

    def weight(o):
        span = pl.ds(o * cap, cap)
        mine = plocal[0, :, span]
        other = premote[0, :, span]
        if o == 4:
            other = mine + 1 + other
            other = jnp.where(other >= mols, other - mols, other)
        scale = pscale[0, :, span]
        high = scale.astype(BF16).astype(F32)
        low = scale - high
        hit = ids == mine
        own = jnp.concatenate([jnp.where(hit, high, 0.0), jnp.where(hit, low, 0.0)], axis=0).astype(BF16)
        far = jnp.where(ids == other, 1.0, 0.0)
        far = jnp.concatenate([far] * (LANES // mols), axis=0).astype(BF16)
        both = lax.dot_general(own, far, NT, preferred_element_type=F32)
        return (both[:mols] + both[mols:]) * norm

    for place, o in enumerate((7, 6, 8, 2, 0)):
        w_send[place] = weight(o)
    w_copies = [
        send(w_send.at[3], w_side.at[0], small_ss.at[1, 0], small_rs.at[1, 0], right),
        send(w_send.at[4], w_side.at[1], small_ss.at[1, 1], small_rs.at[1, 1], left),
        send(w_send.at[pl.ds(0, 3)], w_low, small_ss.at[1, 2], small_rs.at[1, 2], up),
    ]
    for place, o in enumerate((4, 3, 5, 1)):
        w_own[place] = weight(o)

    for a in range(states):
        near[pl.ds(a * mols, mols), :] = rho[0, 0, :, pl.ds(a * aux, aux)]

    def project(start, rows):
        @pl.loop(0, aux // 256)
        def _(i):
            cols = pl.ds(pl.multiple_of(i * 256, 256), 256)
            proj[pl.ds(start, rows), cols] = jnp.dot(
                near[pl.ds(start, rows), :], metric[:, cols], preferred_element_type=F32
            ).astype(BF16)

    def couple(out, out_start, proj_slot, near_start, w):
        dense = lax.dot_general(
            proj[pl.ds(proj_slot * width, width), :],
            near[pl.ds(near_start, tile), :],
            NT, preferred_element_type=F32,
        )
        wide = jnp.concatenate([w] * (tile // LANES), axis=1)
        dense = dense.reshape(states, mols, tile) * wide[None]
        out[:, pl.ds(out_start, tile)] = dense.reshape(width, tile).astype(BF16)

    project(0, width)

    @pl.loop(0, 2)
    def _(h):
        start = pl.multiple_of(h * tile, tile)
        couple(c_own, start, 0, start, w_own[0])

    def stacked(y):
        return jnp.concatenate([y[:, a * vecs:(a + 1) * vecs] for a in range(states)], axis=0)

    def merged(z):
        return jnp.concatenate([z[a * mols:(a + 1) * mols] for a in range(states)], axis=1)

    start_vecs = trial[0, 0].astype(F32)
    ycat[pl.ds(0, width), :] = stacked(start_vecs).astype(BF16)
    e = energy[0, 0]
    e_wide = jnp.concatenate(
        [jnp.broadcast_to(e[:, a:a + 1], (mols, vecs)) for a in range(states)], axis=1
    )
    for slot in range(3):
        y_copies[slot].wait_recv()
        ycat[pl.ds((slot + 1) * width, width), :] = stacked(y_near[slot].astype(F32)).astype(BF16)

    half = states // 2
    for h in range(2):
        for slot in range(3):
            for a in range(h * half, (h + 1) * half):
                rho_copies[slot][a].wait_recv()
            begin = (slot + 1) * width + h * tile
            project(begin, tile)
            couple(c_own, begin, 0, begin, w_own[slot + 1])
    for copy in w_copies:
        copy.wait_recv()

    @pl.loop(0, 6)
    def _(j):
        start = pl.multiple_of(j * tile, tile)
        couple(c_low, start, 3, start, w_low[j // 2])

    @pl.loop(0, 2)
    def _(h):
        start = pl.multiple_of(h * tile, tile)
        source = pl.multiple_of(3 * width + h * tile, tile)
        couple(c_left, start, 1, source, w_side[0])
        couple(c_right, start, 2, source, w_side[1])

    def apply(turn):
        for_low = jnp.dot(c_low[...], ycat[pl.ds(0, 3 * width), :], preferred_element_type=F32)
        last = ycat[pl.ds(3 * width, width), :]
        for_left = jnp.dot(c_left[...], last, preferred_element_type=F32)
        for_right = jnp.dot(c_right[...], last, preferred_element_type=F32)
        parts = [merged(for_left), merged(for_right), merged(for_low)]
        copies = []
        for slot, target in enumerate((left, right, down)):
            ret_send[turn, slot] = parts[slot]
            copies.append(send(
                ret_send.at[turn, slot], ret_near.at[turn, slot],
                small_ss.at[2 + turn, slot], small_rs.at[2 + turn, slot], target,
            ))
        own = merged(jnp.dot(c_own[...], ycat[...], preferred_element_type=F32))
        return own, parts, copies

    def total(turn, rows):
        block = jnp.concatenate(rows + [jnp.zeros((8 - len(rows), rows[0].shape[1]), F32)], axis=0)
        part = sum(block[:, i * LANES:(i + 1) * LANES] for i in range(block.shape[1] // LANES))
        shift = LANES // 2
        while shift >= vecs:
            part = part + pltpu.roll(part, shift, 1)
            shift //= 2
        for buf, ss, rs, me, count, at in (
            (sum_y, ysum_ss, ysum_rs, me_y, ny, lambda i: (me_x, i)),
            (sum_x, xsum_ss, xsum_rs, me_x, nx, lambda i: (i, me_y)),
        ):
            buf[turn, me] = part
            for k in range(1, count):
                send(buf.at[turn, me], buf.at[turn, me], ss.at[turn, k], rs.at[turn, me], at(lax.rem(me + k, count)))
            for k in range(1, count):
                source = lax.rem(me + k, count)
                pltpu.make_async_remote_copy(
                    src_ref=buf.at[turn, me], dst_ref=buf.at[turn, source],
                    send_sem=ss.at[turn, k], recv_sem=rs.at[turn, source],
                    device_id=at(source), device_id_type=MESH,
                ).wait_recv()
            part = buf[turn, 0]
            for i in range(1, count):
                part = part + buf[turn, i]
        return part

    def spread(row):
        return jnp.concatenate([row] * (states * vecs // LANES), axis=1)

    def over_mols(x):
        return jnp.sum(x, axis=0, keepdims=True)

    own, parts, copies = apply(0)
    own = own + e_wide * start_vecs
    inner = start_vecs * own
    for slot in range(3):
        inner = inner + y_near[slot].astype(F32) * parts[slot]
    sums = total(0, [over_mols(inner), over_mols(start_vecs * start_vecs)])
    theta = sums[0:1] / sums[1:2]
    theta_out[...] = theta[:, :vecs]
    theta = spread(theta)
    for slot in range(3):
        copies[slot].wait_recv()
        own = own + ret_near[0, slot]
    sigma_first[0, 0] = own
    resid = (own - theta * start_vecs) / jnp.maximum(jnp.abs(e_wide - theta), 1.0)
    r_send[...] = resid
    r_copies = [
        send(r_send, r_near.at[slot], small_ss.at[4, slot], small_rs.at[4, slot], target)
        for target, slot in routes
    ]
    sums = total(1, [over_mols(resid * resid)])
    factor = spread(1.0 / jnp.sqrt(sums[0:1] / (width * nx * ny) + 1e-6))
    corr = (resid * factor).astype(BF16)
    corr_out[0, 0] = corr
    corr = corr.astype(F32)
    ycat[pl.ds(0, width), :] = stacked(corr).astype(BF16)
    for slot in range(3):
        r_copies[slot].wait_recv()
        ycat[pl.ds((slot + 1) * width, width), :] = stacked(r_near[slot] * factor).astype(BF16)
    own, parts, copies = apply(1)
    own = own + e_wide * corr
    for slot in range(3):
        copies[slot].wait_recv()
        own = own + ret_near[1, slot]
    sigma_second[0, 0] = own
    for copy in pending:
        copy.wait_send()


def shards(densities, trials, energies, metric, pair_local, pair_remote, pair_scale):
    nx, ny = lax.axis_size("gx"), lax.axis_size("gy")
    mols = densities.shape[2]
    states = energies.shape[3]
    aux = metric.shape[0]
    vecs = trials.shape[3] // states
    width = mols * states
    field = (mols, states * vecs)
    vmem = pl.BlockSpec(memory_space=pltpu.VMEM)
    dma = pltpu.SemaphoreType.DMA
    s1, corr, s2, theta = pl.pallas_call(
        functools.partial(kernel, nx, ny),
        out_shape=(
            jax.ShapeDtypeStruct((1, 1) + field, F32),
            jax.ShapeDtypeStruct((1, 1) + field, BF16),
            jax.ShapeDtypeStruct((1, 1) + field, F32),
            jax.ShapeDtypeStruct((1, vecs), F32),
        ),
        in_specs=[vmem] * 7,
        out_specs=(vmem,) * 4,
        scratch_shapes=[
            pltpu.VMEM((4 * width, aux), BF16),
            pltpu.VMEM((4 * width, aux), BF16),
            pltpu.VMEM((width, 4 * width), BF16),
            pltpu.VMEM((width, 3 * width), BF16),
            pltpu.VMEM((width, width), BF16),
            pltpu.VMEM((width, width), BF16),
            pltpu.VMEM((4, mols, LANES), F32),
            pltpu.VMEM((5, mols, LANES), F32),
            pltpu.VMEM((3, mols, LANES), F32),
            pltpu.VMEM((2, mols, LANES), F32),
            pltpu.VMEM((3,) + field, BF16),
            pltpu.VMEM(field, F32),
            pltpu.VMEM((3,) + field, F32),
            pltpu.VMEM((4 * width, vecs), BF16),
            pltpu.VMEM((2, 3) + field, F32),
            pltpu.VMEM((2, 3) + field, F32),
            pltpu.VMEM((2, ny, 8, LANES), F32),
            pltpu.VMEM((2, nx, 8, LANES), F32),
            dma((3, states)), dma((3, states)),
            dma((5, 3)), dma((5, 3)),
            dma((2, ny)), dma((2, ny)),
            dma((2, nx)), dma((2, nx)),
        ],
        compiler_params=pltpu.CompilerParams(
            collective_id=0, has_side_effects=True, vmem_limit_bytes=48 * 1024 * 1024
        ),
    )(densities, trials, energies, metric, pair_local, pair_remote, pair_scale)
    return s1, corr, s2, theta.reshape(vecs)


def solution(mesh):
    field = P("gx", "gy", None, None)
    pair = P("gx", "gy", None)
    return jax.shard_map(
        shards,
        mesh=mesh,
        in_specs=(field, field, field, P(), pair, pair, pair),
        out_specs=(field, field, field, P()),
        check_vma=False,
    )
```

time: 488 us -> 72.2 us (0.15)
  local copies, waits for them, and re-layouts: 229 us -> 8.96 us
  waiting for transfers between devices: 103 us -> 0 us
  blocking collectives: 81.9 us -> 0 us
  Pallas kernels: 0 us -> 62.1 us
  matrix products: 38.4 us -> 0 us
  starting transfers between devices: 21.6 us -> 0 us
  other arithmetic: 10.5 us -> 0 us
    mul x37 -> x0, local copies, waits for them, and re-layouts: 188 us -> none  [the longest x36 188 us: couple(): dense = dense.reshape(mols, states, mols, states) * weight[:, None, :, None]]
    ppermute x12 -> x0, waiting for transfers between devices: 103 us -> none  [the longest x6 100 us: extended(): lax.ppermute(lax.slice_in_dim(block, block.shape[dim] - width, None, axis...]
    psum x2 -> x0, blocking collectives: 81.9 us -> none  [the longest x1 41.5 us: shards(): lax.psum((jnp.sum(start_vecs * sigma_first, axis=(0, 1)), jnp.sum(start_v...]
    pallas_call x0 -> x1, Pallas kernels: none -> 62.1 us  [shards(): pl.pallas_call(functools.partial(kernel, nx, ny), out_shape=(jax.ShapeDty...]
    dot_general x13 -> x0, matrix products: 38.4 us -> none  [the longest x9 17.7 us: couple(): lax.dot_general(proj, far_block, (((1,), (1,)), ((), ())), preferred_elem...]
    ppermute x12 -> x0, starting transfers between devices: 21.6 us -> none  [the longest x6 13.8 us: extended(): lax.ppermute(lax.slice_in_dim(block, 0, width, axis=dim), axis, backward)]
    reshape x4 -> x0, local copies, waits for them, and re-layouts: 18.3 us -> none  [the longest x1 15 us: shards(): near_rho = halo_rho.reshape(9, width, aux)]
    dynamic_update_slice x18 -> x0, local copies, waits for them, and re-layouts: 12.7 us -> none  [shards(): coupled = lax.map(couple, (near_rho, weights))]
  transfers between devices with their start and end apart: 12 -> 0, of which waited for: 7 -> 0; matrix products, arithmetic and copies ran while one was open for 3% -> 0% of each run, Pallas kernels for 0% -> 0%
where the time goes in v1:
time: 72.2 us; the launch traced here: 71.7 us
  Pallas kernels  62.1 us (86%)
  local copies, waits for them, and re-layouts  8.96 us (12%)
    pallas_call x1, Pallas kernels, shards(): pl.pallas_call(functools.partial(kernel, nx, ny), out_shape=(jax.ShapeDty...  62.1 us
    unnamed x17, local copies, waits for them, and re-layouts  8.96 us

profile of v1, /device:TPU:0, one launch (start us, length us, event | category | flops | bytes accessed | tf_op | source)
XLA Modules:
  0.0 71.7 jit_solution(4745523496833717324)
XLA Ops:
  0.6 0.8 %copy.11.energy = f32[1,1,64,8]{3,2,1,0:T(8,128)S(1)} copy(f32[1,1,64,8]{2,3,1,0:T(8,128)} %param.9) | data formatting | bytes 4096 | tf_op args[2]
  1.4 0.0 copy-start
  1.4 1.6 %copy-done = bf16[1024,1024]{1,0:T(8,128)(2,1)S(1)} copy-done((bf16[1024,1024]{1,0:T(8,128)(2,1)S(1)}, bf16[1024,1024]{1,0:T(8,128)(2,1)}, u32[]{:S(2)}) %copy-start) | copy-done | bytes 2097176
  3.0 0.0 copy-start.1
  3.0 1.2 %copy-done.1 = bf16[1,1,64,8192]{3,2,1,0:T(8,128)(2,1)S(1)} copy-done((bf16[1,1,64,8192]{3,2,1,0:T(8,128)(2,1)S(1)}, bf16[1,1,64,8192]{3,2,1,0:T(8,128)(2,1)}, u32[]{:S(2)}) %copy-start.1) | copy-done | bytes 1048600
  4.2 0.0 copy-start.2
  4.2 0.8 %copy-done.2 = bf16[1,1,64,256]{3,2,1,0:T(8,128)(2,1)S(1)} copy-done((bf16[1,1,64,256]{3,2,1,0:T(8,128)(2,1)S(1)}, bf16[1,1,64,256]{3,2,1,0:T(8,128)(2,1)}, u32[]{:S(2)}) %copy-start.2) | copy-done | bytes 32792
  5.0 0.0 copy-start.3
  5.0 0.7 %copy-done.3 = s32[1,1,6912]{2,1,0:T(1,128)S(1)} copy-done((s32[1,1,6912]{2,1,0:T(1,128)S(1)}, s32[1,1,6912]{2,1,0:T(1,128)}, u32[]{:S(2)}) %copy-start.3) | copy-done | bytes 27672
  5.7 0.0 copy-start.4
  5.7 0.7 %copy-done.4 = s32[1,1,6912]{2,1,0:T(1,128)S(1)} copy-done((s32[1,1,6912]{2,1,0:T(1,128)S(1)}, s32[1,1,6912]{2,1,0:T(1,128)}, u32[]{:S(2)}) %copy-start.4) | copy-done | bytes 27672
  6.5 0.0 copy-start.5
  6.5 0.7 %copy-done.5 = f32[1,1,6912]{2,1,0:T(1,128)S(1)} copy-done((f32[1,1,6912]{2,1,0:T(1,128)S(1)}, f32[1,1,6912]{2,1,0:T(1,128)}, u32[]{:S(2)}) %copy-start.5) | copy-done | bytes 27672
  7.2 62.1 %shard_map.102 = (f32[1,1,64,256]{3,2,1,0:T(8,128)S(1)}, bf16[1,1,64,256]{3,2,1,0:T(8,128)(2,1)S(1)}, f32[1,1,64,256]{3,2,1,0:T(8,128)S(1)}, f32[1,32]{1,0:T(1,128)S(1)}) custom-call(bf16[1,1,64,8192]{3,2,1,0:T(8,128)(2,1)S(1)} %copy-done.1, bf16[1,1,64,256]{3,2,1,0:T(8,128)(2,1)S(1)} %copy-done.2, f32[1,1,64,8]{3,2,1,0:T(8,128)S(1)} %copy.11.energy, ...), custom_call_target="tpu_custom_call" | custom-call | tf_op jit(solution)/shard_map/pallas_call | solution.py:263
  69.4 0.6 copy.16
  70.0 0.6 copy.17
  70.6 0.6 copy.18
  71.2 0.5 copy.19
Async XLA Ops:
  1.4 1.6 %copy-start = (bf16[1024,1024]{1,0:T(8,128)(2,1)S(1)}, bf16[1024,1024]{1,0:T(8,128)(2,1)}, u32[]{:S(2)}) copy-start(bf16[1024,1024]{1,0:T(8,128)(2,1)} %metric.1) | copy-start | bytes 6291460
  3.0 1.2 %copy-start.1 = (bf16[1,1,64,8192]{3,2,1,0:T(8,128)(2,1)S(1)}, bf16[1,1,64,8192]{3,2,1,0:T(8,128)(2,1)}, u32[]{:S(2)}) copy-start(bf16[1,1,64,8192]{3,2,1,0:T(8,128)(2,1)} %rho.1) | copy-start | bytes 3145732
  4.2 0.8 %copy-start.2 = (bf16[1,1,64,256]{3,2,1,0:T(8,128)(2,1)S(1)}, bf16[1,1,64,256]{3,2,1,0:T(8,128)(2,1)}, u32[]{:S(2)}) copy-start(bf16[1,1,64,256]{3,2,1,0:T(8,128)(2,1)} %trial.1) | copy-start | bytes 98308
  5.0 0.7 %copy-start.3 = (s32[1,1,6912]{2,1,0:T(1,128)S(1)}, s32[1,1,6912]{2,1,0:T(1,128)}, u32[]{:S(2)}) copy-start(s32[1,1,6912]{2,1,0:T(1,128)} %plocal.1) | copy-start | bytes 82948
  5.7 0.7 %copy-start.4 = (s32[1,1,6912]{2,1,0:T(1,128)S(1)}, s32[1,1,6912]{2,1,0:T(1,128)}, u32[]{:S(2)}) copy-start(s32[1,1,6912]{2,1,0:T(1,128)} %premote.1) | copy-start | bytes 82948
  6.5 0.7 %copy-start.5 = (f32[1,1,6912]{2,1,0:T(1,128)S(1)}, f32[1,1,6912]{2,1,0:T(1,128)}, u32[]{:S(2)}) copy-start(f32[1,1,6912]{2,1,0:T(1,128)} %pscale.1) | copy-start | bytes 82948

commit v2 on v1

--- a/solution.py
+++ b/solution.py
@@ -16,20 +16,21 @@
 
 def kernel(
     nx, ny,
-    rho, trial, energy, metric, plocal, premote, pscale,
+    rho_hbm, trial_hbm, energy_hbm, metric_hbm, plocal_hbm, premote_hbm, pscale_hbm,
     sigma_first, corr_out, sigma_second, theta_out,
-    near, proj, c_own, c_low, c_left, c_right,
+    near, proj, c_own, c_low, c_side,
+    trial, energy, metric, plocal, premote, pscale,
     w_own, w_send, w_low, w_side,
-    y_near, r_send, r_near, ycat, ret_send, ret_near, sum_y, sum_x,
-    rho_ss, rho_rs, small_ss, small_rs, ysum_ss, ysum_rs, xsum_ss, xsum_rs,
+    y_near, r_send, r_near, ycat, ret_send, ret_near, last_send, last_near, sum_y, sum_x,
+    rho_ss, rho_rs, small_ss, small_rs, ysum_ss, ysum_rs, xsum_ss, xsum_rs, load_s, own_s,
 ):
-    mols, full = rho.shape[2], rho.shape[3]
+    mols, full = rho_hbm.shape[2], rho_hbm.shape[3]
     aux = metric.shape[0]
     states = full // aux
+    tile = c_side.shape[1] // 2
     vecs = trial.shape[3] // states
     width = mols * states
     cap = plocal.shape[2] // 9
-    tile = c_left.shape[1] // 2
     me_x, me_y = lax.axis_index("gx"), lax.axis_index("gy")
     up = (lax.rem(me_x + 1, nx), me_y)
     down = (lax.rem(me_x + nx - 1, nx), me_y)
@@ -42,6 +43,22 @@
         pl.semaphore_signal(barrier, inc=1, device_id=(me_x, lax.rem(me_y + k, ny)), device_id_type=MESH)
     for k in range(1, nx):
         pl.semaphore_signal(barrier, inc=1, device_id=(lax.rem(me_x + k, nx), me_y), device_id_type=MESH)
+
+    loads = [
+        pltpu.make_async_copy(src, dst, load_s.at[i])
+        for i, (src, dst) in enumerate((
+            (plocal_hbm, plocal), (premote_hbm, premote), (pscale_hbm, pscale),
+            (trial_hbm, trial), (energy_hbm, energy), (metric_hbm, metric),
+        ))
+    ]
+    own_loads = [
+        pltpu.make_async_copy(
+            rho_hbm.at[0, 0, :, pl.ds(a * aux, aux)], near.at[pl.ds(a * mols, mols), :], own_s.at[a]
+        )
+        for a in range(states)
+    ]
+    for load in own_loads + loads:
+        load.start()
     pl.semaphore_wait(barrier, nx + ny - 2)
 
     pending = []
@@ -55,18 +72,21 @@
         return copy
 
     y_copies = [
-        send(trial.at[0, 0], y_near.at[slot], small_ss.at[0, slot], small_rs.at[0, slot], target)
+        send(trial_hbm.at[0, 0], y_near.at[slot], small_ss.at[0, slot], small_rs.at[0, slot], target)
         for target, slot in routes
     ]
     rho_copies = [[None] * states for _ in range(3)]
     for a in range(states):
+        own_loads[a].wait()
         for target, slot in routes:
             rho_copies[slot][a] = send(
-                rho.at[0, 0, :, pl.ds(a * aux, aux)],
+                near.at[pl.ds(a * mols, mols), :],
                 near.at[pl.ds((slot + 1) * width + a * mols, mols), :],
                 rho_ss.at[slot, a], rho_rs.at[slot, a], target,
             )
 
+    for load in loads[:3]:
+        load.wait()
     norm = 1.0 / (float(aux) ** 0.5)
     ids = lax.broadcasted_iota(jnp.int32, (mols, cap), 0)
 
@@ -97,8 +117,8 @@
     for place, o in enumerate((4, 3, 5, 1)):
         w_own[place] = weight(o)
 
-    for a in range(states):
-        near[pl.ds(a * mols, mols), :] = rho[0, 0, :, pl.ds(a * aux, aux)]
+    for load in loads[3:]:
+        load.wait()
 
     def project(start, rows):
         @pl.loop(0, aux // 256)
@@ -133,7 +153,7 @@
 
     start_vecs = trial[0, 0].astype(F32)
     ycat[pl.ds(0, width), :] = stacked(start_vecs).astype(BF16)
-    e = energy[0, 0]
+    e = energy[0, 0].T
     e_wide = jnp.concatenate(
         [jnp.broadcast_to(e[:, a:a + 1], (mols, vecs)) for a in range(states)], axis=1
     )
@@ -161,20 +181,21 @@
     def _(h):
         start = pl.multiple_of(h * tile, tile)
         source = pl.multiple_of(3 * width + h * tile, tile)
-        couple(c_left, start, 1, source, w_side[0])
-        couple(c_right, start, 2, source, w_side[1])
+        couple(c_side.at[0], start, 1, source, w_side[0])
+        couple(c_side.at[1], start, 2, source, w_side[1])
 
     def apply(turn):
         for_low = jnp.dot(c_low[...], ycat[pl.ds(0, 3 * width), :], preferred_element_type=F32)
         last = ycat[pl.ds(3 * width, width), :]
-        for_left = jnp.dot(c_left[...], last, preferred_element_type=F32)
-        for_right = jnp.dot(c_right[...], last, preferred_element_type=F32)
+        for_left = jnp.dot(c_side[0], last, preferred_element_type=F32)
+        for_right = jnp.dot(c_side[1], last, preferred_element_type=F32)
         parts = [merged(for_left), merged(for_right), merged(for_low)]
         copies = []
         for slot, target in enumerate((left, right, down)):
-            ret_send[turn, slot] = parts[slot]
+            src, dst = ((ret_send, ret_near), (last_send, last_near))[turn]
+            src[slot] = parts[slot].astype(src.dtype)
             copies.append(send(
-                ret_send.at[turn, slot], ret_near.at[turn, slot],
+                src.at[slot], dst.at[slot],
                 small_ss.at[2 + turn, slot], small_rs.at[2 + turn, slot], target,
             ))
         own = merged(jnp.dot(c_own[...], ycat[...], preferred_element_type=F32))
@@ -223,7 +244,7 @@
     theta = spread(theta)
     for slot in range(3):
         copies[slot].wait_recv()
-        own = own + ret_near[0, slot]
+        own = own + ret_near[slot]
     sigma_first[0, 0] = own
     resid = (own - theta * start_vecs) / jnp.maximum(jnp.abs(e_wide - theta), 1.0)
     r_send[...] = resid
@@ -244,7 +265,7 @@
     own = own + e_wide * corr
     for slot in range(3):
         copies[slot].wait_recv()
-        own = own + ret_near[1, slot]
+        own = own + last_near[slot].astype(F32)
     sigma_second[0, 0] = own
     for copy in pending:
         copy.wait_send()
@@ -259,6 +280,8 @@
     width = mols * states
     field = (mols, states * vecs)
     vmem = pl.BlockSpec(memory_space=pltpu.VMEM)
+    hbm = pl.BlockSpec(memory_space=pltpu.HBM)
+    flipped = jnp.swapaxes(energies, 2, 3)
     dma = pltpu.SemaphoreType.DMA
     s1, corr, s2, theta = pl.pallas_call(
         functools.partial(kernel, nx, ny),
@@ -268,15 +291,20 @@
             jax.ShapeDtypeStruct((1, 1) + field, F32),
             jax.ShapeDtypeStruct((1, vecs), F32),
         ),
-        in_specs=[vmem] * 7,
+        in_specs=[hbm] * 7,
         out_specs=(vmem,) * 4,
         scratch_shapes=[
             pltpu.VMEM((4 * width, aux), BF16),
             pltpu.VMEM((4 * width, aux), BF16),
             pltpu.VMEM((width, 4 * width), BF16),
             pltpu.VMEM((width, 3 * width), BF16),
-            pltpu.VMEM((width, width), BF16),
-            pltpu.VMEM((width, width), BF16),
+            pltpu.VMEM((2, width, width), BF16),
+            pltpu.VMEM(trials.shape, trials.dtype),
+            pltpu.VMEM(flipped.shape, flipped.dtype),
+            pltpu.VMEM(metric.shape, metric.dtype),
+            pltpu.VMEM(pair_local.shape, pair_local.dtype),
+            pltpu.VMEM(pair_remote.shape, pair_remote.dtype),
+            pltpu.VMEM(pair_scale.shape, pair_scale.dtype),
             pltpu.VMEM((4, mols, LANES), F32),
             pltpu.VMEM((5, mols, LANES), F32),
             pltpu.VMEM((3, mols, LANES), F32),
@@ -285,19 +313,22 @@
             pltpu.VMEM(field, F32),
             pltpu.VMEM((3,) + field, F32),
             pltpu.VMEM((4 * width, vecs), BF16),
-            pltpu.VMEM((2, 3) + field, F32),
-            pltpu.VMEM((2, 3) + field, F32),
+            pltpu.VMEM((3,) + field, F32),
+            pltpu.VMEM((3,) + field, F32),
+            pltpu.VMEM((3,) + field, BF16),
+            pltpu.VMEM((3,) + field, BF16),
             pltpu.VMEM((2, ny, 8, LANES), F32),
             pltpu.VMEM((2, nx, 8, LANES), F32),
             dma((3, states)), dma((3, states)),
             dma((5, 3)), dma((5, 3)),
             dma((2, ny)), dma((2, ny)),
             dma((2, nx)), dma((2, nx)),
+            dma((6,)), dma((states,)),
         ],
         compiler_params=pltpu.CompilerParams(
-            collective_id=0, has_side_effects=True, vmem_limit_bytes=48 * 1024 * 1024
+            collective_id=0, has_side_effects=True, vmem_limit_bytes=62 * 1024 * 1024
         ),
-    )(densities, trials, energies, metric, pair_local, pair_remote, pair_scale)
+    )(densities, trials, flipped, metric, pair_local, pair_remote, pair_scale)
     return s1, corr, s2, theta.reshape(vecs)
 
 

time: 72.2 us -> 69.2 us (0.958)
  local copies, waits for them, and re-layouts: 8.96 us -> 5.45 us
    unnamed x17 -> x4, local copies, waits for them, and re-layouts: 8.96 us -> 5.45 us
where the time goes in v2:
time: 69.2 us; the launch traced here: 68.9 us
  Pallas kernels  62.8 us (91%)
  local copies, waits for them, and re-layouts  5.45 us (8%)
    pallas_call x1, Pallas kernels, shards(): pl.pallas_call(functools.partial(kernel, nx, ny), out_shape=(jax.ShapeDty...  62.8 us
    unnamed x4, local copies, waits for them, and re-layouts  5.45 us

profile of v2, /device:TPU:0, one launch (start us, length us, event | category | flops | bytes accessed | tf_op | source)
XLA Modules:
  0.0 68.9 jit_solution(2432624596499590577)
XLA Ops:
  0.6 62.8 %shard_map.102 = (f32[1,1,64,256]{3,2,1,0:T(8,128)}, bf16[1,1,64,256]{3,2,1,0:T(8,128)(2,1)}, f32[1,1,64,256]{3,2,1,0:T(8,128)}, f32[1,32]{1,0:T(1,128)}) custom-call(bf16[1,1,64,8192]{3,2,1,0:T(8,128)(2,1)} %rho_hbm.1, bf16[1,1,64,256]{3,2,1,0:T(8,128)(2,1)} %trial_hbm.1, f32[1,1,8,64]{3,2,1,0:T(8,128)} %bitcast.2, bf16[1024,1024]{1,0:T(8,128)(2,1)} %metric_hbm.1, ...), custom_call_target="tpu_custom_call" | custom-call | tf_op jit(solution)/shard_map/pallas_call | solution.py:286
  63.5 1.5 %copy.15 = f32[1,1,64,256]{3,2,1,0:T(8,128)} copy(f32[1,1,64,256]{3,2,1,0:T(8,128)} %get-tuple-element.16) | data formatting | bytes 131072
  64.9 1.4 %copy.16 = bf16[1,1,64,256]{3,2,1,0:T(8,128)(2,1)} copy(bf16[1,1,64,256]{3,2,1,0:T(8,128)(2,1)} %get-tuple-element.17) | data formatting | bytes 65536
  66.3 1.5 %copy.17 = f32[1,1,64,256]{3,2,1,0:T(8,128)} copy(f32[1,1,64,256]{3,2,1,0:T(8,128)} %get-tuple-element.18) | data formatting | bytes 131072
  67.8 1.1 %copy.18 = f32[32]{0:T(128)} copy(f32[32]{0:T(128)} %bitcast.3) | data formatting | bytes 256
